TPU v7x, 32 devices: a whole 2x2x4 slice. The times are simulated.
32 devices in a mesh: lat: 8 (over z, x), lev: 4 (over y, core).
Axes of the slice: x: 2, y: 2, z: 4, core: 2. Of those that a mesh axis runs over, the one named last changes fastest.
Arguments:
- particle_mass_fraction: float32 [20, 64, 8, 360], P(None, 'lat', 'lev'), may hold values from 0.1 to 2
- meridional_cfl_factor: float32 [64, 8, 360], P('lat', 'lev'), may hold values from -0.45 to 0.45
- thermal_state_kelvins: float32 [64, 8, 360], P('lat', 'lev'), may hold values from 200 to 300
- logarithmic_barometric_span: float32 [8], P('lev'), may hold values from 0.06 to 0.2
- gravitational_fall_kilometres: float32 [20], replicated, may hold values from 0.02 to 20
- zonal_cfl_factor: float32 [64, 8, 360], P('lat', None, 'lev'), may hold values from -0.45 to 0.45
- collision_rate_matrix: float32 [20, 20], replicated, may hold values from 0.02 to 0.2
Outputs:
- dust_out: float32 [20, 64, 8, 360], P(None, 'lat', None, 'lev')
- height: float32 [64, 8, 360], P('lat', 'lev')
All inputs are finite; a program needn't handle non-finite values.
Results may differ from a plain program's by a relative error of at most 0.000067.
Values sent between devices are 32-bit elements; how exact they have to be, the bound alone decides.
A program may use at most 128 MiB of HBM per device.

v0:
```python
import jax
import jax.numpy as jnp
from jax import lax
from jax.sharding import PartitionSpec as P

specific_air_factor = 0.0293
scale_height = 7.0


def extended_2(x, sides, width, wrap):
    for axis, dim in sides:
        peers, length = (lax.axis_size(axis), x.shape[dim])
        up = [(i, (i + 1) % peers) for i in range(peers if wrap else peers - 1)]
        down = [(j, i) for i, j in up]
        last = lax.slice_in_dim(x, length - width, length, axis=dim)
        leading = lax.slice_in_dim(x, 0, width, axis=dim)
        before = lax.ppermute(last, axis, up)
        after = lax.ppermute(leading, axis, down)
        x = jnp.concatenate([before, x, after], axis=dim)
    return x


def prefix(value, axis, join, neutral):
    count, mine = (lax.axis_size(axis), lax.axis_index(axis))
    pieces = lax.all_gather(value, axis)
    pieces = pieces[::-1]
    mine = count - 1 - mine
    subtotal = jnp.full_like(value, 0) + jnp.asarray(neutral, value.dtype)

    def step(position, subtotal):
        longer = join(subtotal, pieces[position])
        return jnp.where(position < mine, longer, subtotal)

    return lax.fori_loop(0, count - 1, step, subtotal)


def settle_sweep(mixing, settle_rate, inflow):

    def stepper(flux_in, inputs):
        level_mix, level_rate = inputs
        summed = level_mix + flux_in
        return (level_rate / (1.0 + level_rate) * summed, summed / (1.0 + level_rate))

    _, swept = lax.scan(
        stepper, inflow, (jnp.moveaxis(mixing, 2, 0), jnp.moveaxis(settle_rate, 2, 0))
    )
    return jnp.moveaxis(swept, 0, 2)


def add_terms(earlier, later):
    return earlier + later


def on_device(
    particle_mass_fraction,
    meridional_cfl_factor,
    thermal_state_kelvins,
    logarithmic_barometric_span,
    gravitational_fall_kilometres,
    zonal_cfl_factor,
    collision_rate_matrix,
):
    bin_count = particle_mass_fraction.shape[0]
    stacked = jnp.concatenate([particle_mass_fraction, meridional_cfl_factor[None]], 0)
    padded = extended_2(stacked, (("lat", 1),), 1, False)
    rows_below = padded[:bin_count, :-2]
    rows_above = padded[:bin_count, 2:]
    courant_above = padded[bin_count, 2:]
    south_flux = (
        jnp.maximum(meridional_cfl_factor, 0.0) * rows_below
        + jnp.minimum(meridional_cfl_factor, 0.0) * particle_mass_fraction
    )
    north_flux = (
        jnp.maximum(courant_above, 0.0) * particle_mass_fraction
        + jnp.minimum(courant_above, 0.0) * rows_above
    )
    advected = particle_mass_fraction + south_flux - north_flux
    vertical_span_height = (
        specific_air_factor * thermal_state_kelvins * logarithmic_barometric_span[None, :, None]
    )
    column_total = jnp.sum(vertical_span_height, axis=1)
    incoming = prefix(column_total, "lev", add_terms, jnp.zeros_like(column_total))
    height = (
        incoming[:, None, :]
        + jnp.cumsum(vertical_span_height[:, ::-1], axis=1)[:, ::-1]
        - 0.5 * vertical_span_height
    )
    density = jnp.exp(-height / scale_height)
    packed = jnp.concatenate([advected, vertical_span_height[None], density[None]], 0)
    columns = lax.all_to_all(packed, "lev", split_axis=3, concat_axis=2, tiled=True)
    col_thick = columns[bin_count]
    col_density = columns[bin_count + 1]
    settle_rate = gravitational_fall_kilometres[:, None, None, None] / col_thick[None]
    inflow = jnp.zeros((bin_count, columns.shape[1], columns.shape[3]), jnp.float32)
    settled = settle_sweep(columns[:bin_count], settle_rate, inflow)
    extended = extended_2(
        jnp.concatenate([settled, zonal_cfl_factor[None]], 0), (("lev", 3),), 1, True
    )
    west_mix = extended[:bin_count, :, :, :-2]
    east_mix = extended[:bin_count, :, :, 2:]
    courant_east = extended[bin_count, :, :, 2:]
    west_flux = (
        jnp.maximum(zonal_cfl_factor, 0.0) * west_mix + jnp.minimum(zonal_cfl_factor, 0.0) * settled
    )
    east_flux = jnp.maximum(courant_east, 0.0) * settled + jnp.minimum(courant_east, 0.0) * east_mix
    moved = settled + west_flux - east_flux
    merging = jnp.tril(collision_rate_matrix, -1) - jnp.triu(collision_rate_matrix, 1)
    coag_rate = jnp.einsum("bc,clkx->blkx", merging, moved, precision=lax.Precision.HIGHEST)
    return (moved + col_density * moved * coag_rate, height)


def solution(mesh):
    in_specs = (
        P(None, "lat", "lev", None),
        P("lat", "lev", None),
        P("lat", "lev", None),
        P("lev"),
        P(),
        P("lat", None, "lev"),
        P(),
    )
    out_specs = (P(None, "lat", None, "lev"), P("lat", "lev", None))
    return jax.shard_map(
        on_device, mesh=mesh, in_specs=in_specs, out_specs=out_specs, check_vma=False
    )
```

profile of v0, /device:TPU:0, one launch (start us, length us, event | category | flops | bytes accessed | tf_op | source)
XLA Modules:
  0.0 57.4 jit_solution(17528665692314259171)
XLA Ops:
  0.6 0.0 copy-start
  0.6 1.0 %pad_maximum_fusion.11 = (f32[21,1,2,360]{3,2,1,0:T(2,128)S(1)}, f32[21,1,2,360]{3,2,1,0:T(2,128)S(1)}) fusion(f32[1,8,2,360]{3,2,1,0:T(2,128)} %bitcast.67, f32[20,8,2,360]{3,2,1,0:T(2,128)} %param.11), kind=kLoop, calls=%fused_computation.41 | loop fusion | flops 30240 | bytes 604800 | tf_op jit(solution)/shard_map/slice | solution.py:15
  1.7 1.3 %collective-permute-start.1 = (f32[21,1,2,360]{3,2,1,0:T(2,128)S(1)}, f32[21,1,2,360]{3,2,1,0:T(2,128)S(1)}, u32[]{:S(2)}, u32[]{:S(2)}) collective-permute-start(f32[21,1,2,360]{3,2,1,0:T(2,128)S(1)} %get-tuple-element.233), channel_id=1, source_target_pairs={{4,0},{8,4},{12,8},{16,12},{20,16},{24,20},{28,24},{5,1},{9,5},{13... | collective-permute-start | bytes 181448 | tf_op jit(solution)/shard_map/ppermute | solution.py:18
  3.0 5.5 %collective-permute-start = (f32[21,1,2,360]{3,2,1,0:T(2,128)S(1)}, f32[21,1,2,360]{3,2,1,0:T(2,128)S(1)}, u32[]{:S(2)}, u32[]{:S(2)}) collective-permute-start(f32[21,1,2,360]{3,2,1,0:T(2,128)S(1)} %get-tuple-element.232), channel_id=1, source_target_pairs={{0,4},{4,8},{8,12},{12,16},{16,20},{20,24},{24,28},{1,5},{5,9},{9,... | collective-permute-start | bytes 181448 | tf_op jit(solution)/shard_map/ppermute | solution.py:17
  8.4 0.8 %broadcast_maximum_fusion.2 = (f32[8,2,360]{2,1,0:T(2,128)S(1)}, f32[8,2,360]{2,1,0:T(2,128)S(1)}) fusion(f32[8,2,360]{2,1,0:T(2,128)} %param.12), kind=kLoop, calls=%fused_computation.60 | loop fusion | flops 11520 | bytes 69120 | tf_op jit(solution)/shard_map/max | solution.py:70
  9.2 0.7 %broadcast_multiply_fusion = f32[2]{0:T(128)S(1)} fusion(f32[2]{0:T(128)} %param.14), kind=kLoop, calls=%fused_computation.64 | loop fusion | flops 2 | bytes 16 | tf_op jit(solution)/shard_map/mul | solution.py:79
  9.9 0.8 %fusion.29 = (f32[8,360]{1,0:T(8,128)S(1)}, f32[8,2,360]{2,0,1:T(8,128)S(1)}) fusion(f32[2]{0:T(128)S(1)} %broadcast_multiply_fusion, f32[8,2,360]{2,1,0:T(2,128)} %param.13), kind=kLoop, calls=%fused_computation.67 | loop fusion | flops 8640 | bytes 57608 | tf_op jit(solution)/shard_map/reduce_sum | solution.py:81
  10.7 0.1 fusion.31
  10.8 5.3 %all-gather = f32[32,360]{1,0:T(8,128)S(1)} all-gather(f32[8,360]{1,0:T(8,128)S(1)} %get-tuple-element.224), channel_id=2, replica_groups=mesh['lat'=8,'lev'=4] {'lev'}, dimensions={0}, use_global_device_ids=true | all-gather | bytes 57600 | tf_op jit(solution)/shard_map/all_gather | solution.py:25
  16.1 0.1 while.27
  16.2 0.6 %exponential_bitcast_fusion = (f32[1,8,2,360]{3,1,2,0:T(8,128)S(1)}, f32[8,2,360]{2,0,1:T(8,128)}) fusion(f32[8,2,360]{2,0,1:T(8,128)S(1)} %get-tuple-element.225, f32[8,2,360]{2,0,1:T(8,128)S(1)} %fusion.31, f32[8,360]{1,0:T(8,128)S(1)} %get-tuple-element.108), kind=kLoop, calls=%fused_computation.45 | loop fusion | flops 28800 | bytes 103680 | tf_op jit(solution)/shard_map/broadcast_in_dim | solution.py:89
  16.8 0.0 collective-permute-done.1
  16.8 0.8 %maximum_bitcast_fusion = (f32[8,2,360]{2,1,0:T(2,128)S(1)}, f32[1,8,2,360]{3,2,1,0:T(2,128)S(1)}) fusion(f32[21,1,2,360]{3,2,1,0:T(2,128)S(1)} %collective-permute-done.1, f32[1,8,2,360]{3,2,1,0:T(2,128)} %bitcast.68, f32[20,8,2,360]{3,2,1,0:T(2,128)} %param.11), kind=kLoop, calls=%fused_computation.48 | loop fusion | flops 17280 | bytes 590400 | tf_op jit(solution)/shard_map/mul | solution.py:74
  17.7 0.0 collective-permute-done
  17.7 1.7 %pad_maximum_fusion.8 = (f32[20,8,2,360]{3,2,1,0:T(2,128)S(1)}, f32[20,8,2,360]{3,2,1,0:T(2,128)S(1)}) fusion(f32[21,1,2,360]{3,2,1,0:T(2,128)S(1)} %collective-permute-done, f32[1,8,2,360]{3,2,1,0:T(2,128)} %bitcast.69, f32[20,8,2,360]{3,2,1,0:T(2,128)} %param.11, f32[21,1,2,360]{3,2,1,0:T(2,128)S(1)} %collective-permute-done.1), kind=kLoop, calls=%fused_computation.27 | loop fusion | flops 460800 | bytes 1526400 | tf_op jit(solution)/shard_map/concatenate | solution.py:19
  19.4 0.0 copy-done
  19.4 0.1 fusion.14
  19.6 1.3 %copy.255 = f32[22,8,2,360]{0,1,2,3:T(8,128)S(1)} copy(f32[22,8,2,360]{3,1,2,0:T(8,128)S(1)} %pad_maximum_fusion.5) | data formatting | bytes 1013760 | tf_op jit(solution)/shard_map/concatenate | solution.py:89
  20.9 0.0 copy-start.2
  20.9 3.7 %reshape.18 = f32[4,1,31680]{2,1,0:T(1,128)} reshape(f32[360,2,8,22]{3,2,1,0:T(8,128)S(1)} %bitcast.60) | data formatting | bytes 1013760
  24.6 3.5 %all-to-all-start = ((f32[4,1,31680]{2,1,0:T(1,128)}), f32[4,1,31680]{2,1,0:T(1,128)S(1)}, u32[]{:S(2)}, u32[]{:S(2)}) async-start(f32[4,1,31680]{2,1,0:T(1,128)} %reshape.18), calls=%async_computation | async-start | bytes 1015808 | tf_op jit(solution)/shard_map/all_to_all | solution.py:90
  28.1 0.0 copy-done.2
  28.1 0.6 %broadcast_maximum_fusion.1 = (f32[8,8,90]{2,1,0:T(8,128)}, f32[8,8,90]{2,1,0:T(8,128)}) fusion(f32[8,8,90]{2,1,0:T(8,128)S(1)} %copy-done.2), kind=kLoop, calls=%fused_computation.52 | loop fusion | flops 11520 | bytes 69120 | tf_op jit(solution)/shard_map/max | solution.py:103
  28.7 8.1 %all-to-all-done = f32[4,1,31680]{2,1,0:T(1,128)S(1)} async-done(((f32[4,1,31680]{2,1,0:T(1,128)}), f32[4,1,31680]{2,1,0:T(1,128)S(1)}, u32[]{:S(2)}, u32[]{:S(2)}) %all-to-all-start) | async-done | bytes 506912 | tf_op jit(solution)/shard_map/all_to_all | solution.py:90
  36.8 0.6 %broadcast.65 = f32[]{:T(128)} broadcast(f32[]{:T(128)} %constant.131), dimensions={} | broadcast | bytes 8 | tf_op jit(solution)/shard_map/all_to_all | solution.py:90
  37.4 2.2 %reduce = f32[4,31680]{1,0:T(4,128)S(1)} reduce(f32[4,1,31680]{2,1,0:T(1,128)S(1)} %all-to-all-done, f32[]{:T(128)} %broadcast.65), dimensions={1}, to_apply=%all_to_all.11.reduce_sub_computation | reduce | bytes 1013764 | tf_op jit(solution)/shard_map/all_to_all | solution.py:90
  39.6 3.5 %reshape.19 = f32[360,2,8,22]{3,2,1,0:T(8,128)S(1)} reshape(f32[4,31680]{1,0:T(4,128)S(1)} %reduce) | data formatting | bytes 1013760
  43.1 0.0 copy-start.7
  43.1 2.2 %copy.270 = f32[22,8,2,4,90]{4,3,1,2,0:T(4,128)} copy(f32[22,8,2,4,90]{0,1,2,4,3:T(8,128)S(1)} %bitcast.59) | data formatting | bytes 1013760 | tf_op jit(solution)/shard_map/all_to_all | solution.py:90
  45.3 0.0 copy-start.1
  45.3 0.8 %fusion.30 = (f32[1,8,4,2,90]{4,2,1,3,0:T(4,128)S(1)}, f32[1,8,4,2,90]{4,2,1,3,0:T(4,128)S(1)}) fusion(f32[22,8,4,2,90]{4,2,1,3,0:T(4,128)} %bitcast.65), kind=kLoop, calls=%fused_computation.68 | loop fusion | bytes 92160 | tf_op jit(solution)/shard_map/slice | solution.py:92
  46.1 1.1 %slice.65 = f32[20,8,4,2,90]{4,2,1,3,0:T(4,128)S(1)} slice(f32[22,8,4,2,90]{4,2,1,3,0:T(4,128)} %bitcast.66), slice={[0:20], [0:8], [0:4], [0:2], [0:90]} | slice | bytes 921600 | tf_op jit(solution)/shard_map/slice | solution.py:95
  47.3 0.0 copy-start.3
  47.4 0.0 copy-done.7
  47.4 0.1 broadcast_divide_fusion
  47.5 0.0 copy-done.1
  47.5 0.8 %while.28 = (s32[]{:T(128)}, f32[20,8,90]{2,1,0:T(8,128)S(1)}, f32[8,20,8,90]{3,2,1,0:T(8,128)S(1)}, f32[8,20,8,90]{3,2,1,0:T(8,128)S(1)}, f32[8,20,8,90]{3,2,1,0:T(8,128)S(1)}, /*index=5*/s32[]{:T(128)}, s32[]{:T(128)}) while((s32[]{:T(128)}, f32[20,8,90]{2,1,0:T(8,128)S(1)}, f32[8,20,8,90]{3,2,1,0:T(8,128)S(1)}, ...), condition=%wide.region_5.6_spmd.clone, body=%wide.region_4.5_spmd.clone.sunk | while | flops 129603 | bytes 558176 | solution.py:44
  48.3 0.0 copy-start.4
  48.3 0.1 copy.291
  48.5 0.0 copy-done.3
  48.5 0.4 slice_maximum_fusion
  48.8 0.0 copy-start.5
  48.8 0.0 copy-start.6
  48.9 0.0 copy-start.8
  48.9 0.5 copy.263
  49.3 0.0 collective-permute-start.3
  49.4 0.0 copy-done.4
  49.4 0.6 %copy.268 = f32[8,2,360]{2,1,0:T(2,128)} copy(f32[8,2,360]{2,0,1:T(8,128)S(1)} %copy-done.4) | data formatting | bytes 46080
  50.0 0.5 copy.261
  50.5 0.7 %collective-permute-start.2 = (f32[21,8,8,1]{0,2,3,1:T(8,128)S(1)}, f32[21,8,8,1]{0,2,3,1:T(8,128)S(1)}, u32[]{:S(2)}, u32[]{:S(2)}) collective-permute-start(f32[21,8,8,1]{0,2,3,1:T(8,128)S(1)} %copy.261), channel_id=1, source_target_pairs={{0,1},{1,2},{2,3},{3,0},{4,5},{5,6},{6,7},{7,4},{8,9},{9,10},{10,1... | collective-permute-start | bytes 16136 | tf_op jit(solution)/shard_map/ppermute | solution.py:17
  51.2 0.0 collective-permute-done.3
  51.2 0.5 copy.264
  51.7 0.3 broadcast_maximum_fusion
  52.0 2.0 %collective-permute-done.2 = f32[21,8,8,1]{0,2,3,1:T(8,128)S(1)} collective-permute-done((f32[21,8,8,1]{0,2,3,1:T(8,128)S(1)}, f32[21,8,8,1]{0,2,3,1:T(8,128)S(1)}, u32[]{:S(2)}, u32[]{:S(2)}) %collective-permute-start.2) | collective-permute-done | bytes 5408 | tf_op jit(solution)/shard_map/ppermute | solution.py:17
  54.1 0.5 copy.262
  54.6 0.0 copy-done.5
  54.6 0.0 copy-done.6
  54.6 0.0 copy-done.8
  54.6 1.9 %fusion.3 = f32[20,8,8,90]{3,0,2,1:T(8,128)S(1)} fusion(f32[21,8,8,1]{3,0,2,1:T(8,128)S(1)} %copy.264, f32[1,8,8,90]{3,0,2,1:T(1,128)S(1)} %bitcast.73, f32[20,8,8,90]{3,0,2,1:T(8,128)S(1)} %bitcast.63, f32[21,8,8,1]{3,0,2,1:T(8,128)S(1)} %copy.262, f32[8,8,90]{2,1,0:T(8,128)S(1)} %copy.266, f32[8,8,90]{2,1,0:T(8,128)S(1)} %bitcast.78, ...), kind=kOutput, calls=%fused_computation.8 | convolution fusion | flops 30760400 | bytes 1072272 | tf_op jit(solution)/shard_map/bc,clkx->blkx/dot_general | solution.py:108
  56.5 1.0 %copy.267 = f32[20,8,8,90]{3,2,1,0:T(8,128)} copy(f32[20,8,8,90]{3,0,2,1:T(8,128)S(1)} %fusion.3) | data formatting | bytes 921600
  (36 shorter events, 0.7 us)
Async XLA Ops:
  0.6 18.8 %copy-start = (f32[20,8,2,360]{3,2,1,0:T(2,128)S(1)}, f32[20,8,2,360]{3,2,1,0:T(2,128)}, u32[]{:S(2)}) copy-start(f32[20,8,2,360]{3,2,1,0:T(2,128)} %param.11) | copy-start | bytes 1382404
  1.7 15.2 %collective-permute-start.1 = (f32[21,1,2,360]{3,2,1,0:T(2,128)S(1)}, f32[21,1,2,360]{3,2,1,0:T(2,128)S(1)}, u32[]{:S(2)}, u32[]{:S(2)}) collective-permute-start(f32[21,1,2,360]{3,2,1,0:T(2,128)S(1)} %get-tuple-element.233), channel_id=1, source_target_pairs={{4,0},{8,4},{12,8},{16,12},{20,16},{24,20},{28,24},{5,1},{9,5},{13... | collective-permute-start | bytes 181448 | tf_op jit(solution)/shard_map/ppermute | solution.py:18
  3.0 14.7 %collective-permute-start = (f32[21,1,2,360]{3,2,1,0:T(2,128)S(1)}, f32[21,1,2,360]{3,2,1,0:T(2,128)S(1)}, u32[]{:S(2)}, u32[]{:S(2)}) collective-permute-start(f32[21,1,2,360]{3,2,1,0:T(2,128)S(1)} %get-tuple-element.232), channel_id=1, source_target_pairs={{0,4},{4,8},{8,12},{12,16},{16,20},{20,24},{24,28},{1,5},{5,9},{9,... | collective-permute-start | bytes 181448 | tf_op jit(solution)/shard_map/ppermute | solution.py:17
  20.9 7.2 %copy-start.2 = (f32[8,8,90]{2,1,0:T(8,128)S(1)}, f32[8,8,90]{2,1,0:T(8,128)}, u32[]{:S(2)}) copy-start(f32[8,8,90]{2,1,0:T(8,128)} %param.16) | copy-start | bytes 69124
  24.6 12.3 %all-to-all-start = ((f32[4,1,31680]{2,1,0:T(1,128)}), f32[4,1,31680]{2,1,0:T(1,128)S(1)}, u32[]{:S(2)}, u32[]{:S(2)}) async-start(f32[4,1,31680]{2,1,0:T(1,128)} %reshape.18), calls=%async_computation | async-start | bytes 1015808 | tf_op jit(solution)/shard_map/all_to_all | solution.py:90
  43.1 4.3 %copy-start.7 = (f32[20]{0:T(128)S(1)}, f32[20]{0:T(128)}, u32[]{:S(2)}) copy-start(f32[20]{0:T(128)} %param.15) | copy-start | bytes 244
  45.3 2.2 %copy-start.1 = (f32[8,20,8,90]{3,2,1,0:T(8,128)S(1)}, f32[8,20,8,90]{3,2,1,0:T(8,128)}, u32[]{:S(2)}) copy-start(f32[8,20,8,90]{3,2,1,0:T(8,128)} %custom-call.2) | copy-start | bytes 1382404
  47.3 1.1 %copy-start.3 = (f32[8,8,90]{2,1,0:T(8,128)S(1)}, f32[8,8,90]{2,1,0:T(8,128)}, u32[]{:S(2)}) copy-start(f32[8,8,90]{2,1,0:T(8,128)} %param.16) | copy-start | bytes 69124
  48.3 1.1 %copy-start.4 = (f32[8,2,360]{2,0,1:T(8,128)S(1)}, f32[8,2,360]{2,0,1:T(8,128)}, u32[]{:S(2)}) copy-start(f32[8,2,360]{2,0,1:T(8,128)} %get-tuple-element.223) | copy-start | bytes 69124
  48.8 5.7 %copy-start.5 = (f32[8,8,90]{2,1,0:T(8,128)S(1)}, f32[8,8,90]{2,1,0:T(8,128)}, u32[]{:S(2)}) copy-start(f32[8,8,90]{2,1,0:T(8,128)} %get-tuple-element.234) | copy-start | bytes 69124
  48.8 5.7 %copy-start.6 = (f32[8,8,90]{2,1,0:T(8,128)S(1)}, f32[8,8,90]{2,1,0:T(8,128)}, u32[]{:S(2)}) copy-start(f32[8,8,90]{2,1,0:T(8,128)} %get-tuple-element.235) | copy-start | bytes 69124
  48.9 5.7 %copy-start.8 = (f32[20,20]{1,0:T(8,128)S(1)}, f32[20,20]{1,0:T(8,128)}, u32[]{:S(2)}) copy-start(f32[20,20]{1,0:T(8,128)} %param.17) | copy-start | bytes 4804
  49.3 1.9 %collective-permute-start.3 = (f32[21,8,8,1]{0,2,3,1:T(8,128)S(1)}, f32[21,8,8,1]{0,2,3,1:T(8,128)S(1)}, u32[]{:S(2)}, u32[]{:S(2)}) collective-permute-start(f32[21,8,8,1]{0,2,3,1:T(8,128)S(1)} %copy.263), channel_id=1, source_target_pairs={{1,0},{2,1},{3,2},{0,3},{5,4},{6,5},{7,6},{4,7},{9,8},{10,9},{11,1... | collective-permute-start | bytes 16136 | tf_op jit(solution)/shard_map/ppermute | solution.py:18
  50.5 3.5 %collective-permute-start.2 = (f32[21,8,8,1]{0,2,3,1:T(8,128)S(1)}, f32[21,8,8,1]{0,2,3,1:T(8,128)S(1)}, u32[]{:S(2)}, u32[]{:S(2)}) collective-permute-start(f32[21,8,8,1]{0,2,3,1:T(8,128)S(1)} %copy.261), channel_id=1, source_target_pairs={{0,1},{1,2},{2,3},{3,0},{4,5},{5,6},{6,7},{7,4},{8,9},{9,10},{10,1... | collective-permute-start | bytes 16136 | tf_op jit(solution)/shard_map/ppermute | solution.py:17
where the time goes:
time: 57.9 us; the launch traced here: 57.4 us
  local copies, waits for them, and re-layouts  17 us (29%)
  starting transfers between devices  11 us (19%)
  other arithmetic  10.8 us (19%)
  waiting for transfers between devices  10.1 us (17%)
  blocking collectives  5.29 us (9%)
  matrix products  1.89 us (3%)
  between operations  1.01 us (2%)
    unnamed x22, local copies, waits for them, and re-layouts  8.74 us
    all_to_all x1, waiting for transfers between devices, on_device(): lax.all_to_all(packed, 'lev', split_axis=3, concat_axis=2, tiled=True)  8.13 us
    ppermute x2, starting transfers between devices, extended_2(): before = lax.ppermute(last, axis, up)  6.16 us
    all_gather x1, blocking collectives, prefix(): pieces = lax.all_gather(value, axis)  5.29 us
    all_to_all x1, starting transfers between devices, on_device(): lax.all_to_all(packed, 'lev', split_axis=3, concat_axis=2, tiled=True)  3.47 us
    all_to_all x2, local copies, waits for them, and re-layouts, on_device(): lax.all_to_all(packed, 'lev', split_axis=3, concat_axis=2, tiled=True)  2.8 us
    all_to_all x1, other arithmetic, on_device(): lax.all_to_all(packed, 'lev', split_axis=3, concat_axis=2, tiled=True)  2.16 us
    ppermute x2, waiting for transfers between devices, extended_2(): before = lax.ppermute(last, axis, up)  2.01 us
  transfers between devices with their start and end apart: 5, of which 2 were waited for; matrix products, arithmetic and copies ran while one was open for 11% of the time, Pallas kernels for 0%

commit v1 on v0

--- a/solution.py
+++ b/solution.py
@@ -87,7 +87,10 @@
     )
     density = jnp.exp(-height / scale_height)
     packed = jnp.concatenate([advected, vertical_span_height[None], density[None]], 0)
-    columns = lax.all_to_all(packed, "lev", split_axis=3, concat_axis=2, tiled=True)
+    columns = jnp.concatenate(
+        lax.all_to_all(jnp.stack(jnp.split(packed, lax.axis_size("lev"), axis=3)), "lev", 0, 0),
+        axis=2,
+    )
     col_thick = columns[bin_count]
     col_density = columns[bin_count + 1]
     settle_rate = gravitational_fall_kilometres[:, None, None, None] / col_thick[None]

time: 57.9 us -> 42.9 us (0.74)
  the two profiles are of different devices: /device:TPU:0 before, /device:TPU:16 now
where the time goes in v1:
time: 42.9 us; the launch traced here: 42.4 us
  waiting for transfers between devices  12.9 us (30%)
  starting transfers between devices  10.9 us (25%)
  local copies, waits for them, and re-layouts  7.26 us (17%)
  blocking collectives  5.23 us (12%)
  other arithmetic  3 us (7%)
  matrix products  1.88 us (4%)
  between operations  0.95 us (2%)
    all_to_all x1, waiting for transfers between devices, on_device(): lax.all_to_all(jnp.stack(jnp.split(packed, lax.axis_size('lev'), axis=3))...  10.9 us
    all_gather x1, blocking collectives, prefix(): pieces = lax.all_gather(value, axis)  5.23 us
    unnamed x16, local copies, waits for them, and re-layouts  4.74 us
    ppermute x2, starting transfers between devices, extended_2(): before = lax.ppermute(last, axis, up)  3.91 us
    all_to_all x1, starting transfers between devices, on_device(): lax.all_to_all(jnp.stack(jnp.split(packed, lax.axis_size('lev'), axis=3))...  3.62 us
    ppermute x2, starting transfers between devices, extended_2(): after = lax.ppermute(leading, axis, down)  3.37 us
    ppermute x2, waiting for transfers between devices, extended_2(): before = lax.ppermute(last, axis, up)  2.01 us
    dot_general x1, matrix products, on_device(): jnp.einsum('bc,clkx->blkx', merging, moved, precision=lax.Precision.HIGHEST)  1.88 us
  transfers between devices with their start and end apart: 5, of which 2 were waited for; matrix products, arithmetic and copies ran while one was open for 5% of the time, Pallas kernels for 0%

profile of v1, /device:TPU:16, one launch (start us, length us, event | category | flops | bytes accessed | tf_op | source)
XLA Modules:
  0.0 42.4 jit_solution(478763982617535670)
XLA Ops:
  0.6 0.7 %copy.56 = f32[8,2,360]{2,0,1:T(8,128)S(1)} copy(f32[8,2,360]{2,1,0:T(2,128)} %param.12) | data formatting | bytes 46080 | tf_op args[1]
  1.4 1.1 %copy.33 = f32[20,8,2,360]{3,1,2,0:T(8,128)S(1)} copy(f32[20,8,2,360]{3,2,1,0:T(2,128)} %param.11) | data formatting | bytes 921600 | tf_op args[0]
  2.4 0.0 copy-start.1
  2.4 0.1 pad_maximum_fusion.12
  2.5 3.4 %collective-permute-start = (f32[21,1,2,360]{3,1,2,0:T(1,128)S(1)}, f32[21,1,2,360]{3,1,2,0:T(1,128)S(1)}, u32[]{:S(2)}, u32[]{:S(2)}) collective-permute-start(f32[21,1,2,360]{3,1,2,0:T(1,128)S(1)} %get-tuple-element.183), channel_id=1, source_target_pairs={{0,4},{4,8},{8,12},{12,16},{16,20},{20,24},{24,28},{1,5},{5,9},{9,... | collective-permute-start | bytes 181448 | tf_op jit(solution)/shard_map/ppermute | solution.py:17
  5.9 3.3 %collective-permute-start.1 = (f32[21,1,2,360]{3,1,2,0:T(1,128)S(1)}, f32[21,1,2,360]{3,1,2,0:T(1,128)S(1)}, u32[]{:S(2)}, u32[]{:S(2)}) collective-permute-start(f32[21,1,2,360]{3,1,2,0:T(1,128)S(1)} %get-tuple-element.184), channel_id=1, source_target_pairs={{4,0},{8,4},{12,8},{16,12},{20,16},{24,20},{28,24},{5,1},{9,5},{13... | collective-permute-start | bytes 181448 | tf_op jit(solution)/shard_map/ppermute | solution.py:18
  9.3 0.0 copy-done.1
  9.3 0.0 copy-start.2
  9.4 0.0 copy-start.5
  9.4 0.6 %copy-done.5 = f32[2]{0:T(128)S(1)} copy-done((f32[2]{0:T(128)S(1)}, f32[2]{0:T(128)}, u32[]{:S(2)}) %copy-start.5) | copy-done | bytes 32
  10.0 0.0 copy-done.2
  10.1 0.1 fusion.31
  10.1 0.1 fusion.33
  10.3 5.2 %all-gather = f32[32,360]{1,0:T(8,128)S(1)} all-gather(f32[8,360]{1,0:T(8,128)S(1)} %get-tuple-element.173), channel_id=2, replica_groups=mesh['lat'=8,'lev'=4] {'lev'}, dimensions={0}, use_global_device_ids=true | all-gather | bytes 57600 | tf_op jit(solution)/shard_map/all_gather | solution.py:25
  15.5 0.1 while.27
  15.6 0.0 collective-permute-done.1
  15.7 0.0 collective-permute-done
  15.7 0.3 fusion.15
  16.1 0.2 slice_bitcast_fusion.3
  16.3 1.0 %pad_maximum_fusion.5 = f32[4,22,8,2,90]{4,2,3,1,0:T(8,128)} fusion(f32[1,22,8,2,90]{4,2,3,1,0:T(8,128)S(1)} %get-tuple-element.180, f32[1,22,8,2,90]{4,2,3,1,0:T(8,128)S(1)} %get-tuple-element.181, f32[1,22,8,2,90]{4,2,3,1,0:T(8,128)S(1)} %get-tuple-element.182, f32[1,22,8,2,90]{4,2,3,1,0:T(8,128)S(1)} %get-tuple-element.179), kind=kLoop, calls=%fused_computation.24 | loop fusion | flops 380160 | bytes 1013760 | tf_op jit(solution)/shard_map/stack | solution.py:91
  17.2 0.0 copy-start
  17.2 3.6 %all-to-all-start = ((f32[4,22,8,2,90]{4,2,3,1,0:T(8,128)}), f32[4,22,8,2,90]{4,2,3,1,0:T(8,128)S(1)}, u32[]{:S(2)}, u32[]{:S(2)}) async-start(f32[4,22,8,2,90]{4,2,3,1,0:T(8,128)} %pad_maximum_fusion.5), calls=%async_computation | async-start | bytes 1441792 | tf_op jit(solution)/shard_map/all_to_all | solution.py:91
  20.9 0.0 copy-done
  20.9 10.9 %all-to-all-done = f32[4,22,8,2,90]{4,2,3,1,0:T(8,128)S(1)} async-done(((f32[4,22,8,2,90]{4,2,3,1,0:T(8,128)}), f32[4,22,8,2,90]{4,2,3,1,0:T(8,128)S(1)}, u32[]{:S(2)}, u32[]{:S(2)}) %all-to-all-start) | async-done | bytes 506912 | tf_op jit(solution)/shard_map/all_to_all | solution.py:91
  31.8 0.1 copy.54
  31.9 0.1 slice.65
  32.0 0.0 copy-start.3
  32.0 0.6 %copy-done.3 = f32[20]{0:T(128)S(1)} copy-done((f32[20]{0:T(128)S(1)}, f32[20]{0:T(128)}, u32[]{:S(2)}) %copy-start.3) | copy-done | bytes 104
  32.6 0.1 broadcast_divide_fusion
  32.7 0.8 %while.28 = (s32[]{:T(128)}, f32[20,8,90]{2,1,0:T(8,128)S(1)}, f32[8,20,8,90]{3,2,1,0:T(8,128)S(1)}, f32[8,20,8,90]{3,2,1,0:T(8,128)S(1)}, f32[8,20,8,90]{3,2,1,0:T(8,128)S(1)}, /*index=5*/s32[]{:T(128)}, s32[]{:T(128)}) while((s32[]{:T(128)}, f32[20,8,90]{2,1,0:T(8,128)S(1)}, f32[8,20,8,90]{3,2,1,0:T(8,128)S(1)}, ...), condition=%wide.region_5.6_spmd.clone, body=%wide.region_4.5_spmd.clone.sunk | while | flops 129603 | bytes 558184 | solution.py:44
  33.5 0.1 copy.53
  33.7 0.4 slice_maximum_fusion
  34.1 0.5 %copy.41 = f32[21,8,8,1]{0,2,3,1:T(8,128)S(1)} copy(f32[21,8,8,1]{3,0,2,1:T(8,128)S(1)} %get-tuple-element.176) | data formatting | bytes 10752 | tf_op jit(solution)/shard_map/slice | solution.py:16
  34.5 0.0 collective-permute-start.3
  34.6 0.6 %copy.45 = f32[8,2,360]{2,1,0:T(2,128)} copy(f32[8,2,360]{2,0,1:T(8,128)S(1)} %get-tuple-element.172) | data formatting | bytes 46080
  35.2 0.5 %copy.39 = f32[21,8,8,1]{0,2,3,1:T(8,128)S(1)} copy(f32[21,8,8,1]{3,0,2,1:T(8,128)S(1)} %get-tuple-element.175) | data formatting | bytes 10752 | tf_op jit(solution)/shard_map/slice | solution.py:15
  35.7 0.5 %collective-permute-start.2 = (f32[21,8,8,1]{0,2,3,1:T(8,128)S(1)}, f32[21,8,8,1]{0,2,3,1:T(8,128)S(1)}, u32[]{:S(2)}, u32[]{:S(2)}) collective-permute-start(f32[21,8,8,1]{0,2,3,1:T(8,128)S(1)} %copy.39), channel_id=1, source_target_pairs={{0,1},{1,2},{2,3},{3,0},{4,5},{5,6},{6,7},{7,4},{8,9},{9,10},{10,1... | collective-permute-start | bytes 16136 | tf_op jit(solution)/shard_map/ppermute | solution.py:17
  36.2 0.0 collective-permute-done.3
  36.2 0.5 %copy.42 = f32[21,8,8,1]{3,0,2,1:T(8,128)S(1)} copy(f32[21,8,8,1]{0,2,3,1:T(8,128)S(1)} %collective-permute-done.3) | data formatting | bytes 10752 | tf_op jit(solution)/shard_map/ppermute | solution.py:18
  36.7 0.3 broadcast_maximum_fusion
  37.0 0.0 copy-start.4
  37.1 2.0 %collective-permute-done.2 = f32[21,8,8,1]{0,2,3,1:T(8,128)S(1)} collective-permute-done((f32[21,8,8,1]{0,2,3,1:T(8,128)S(1)}, f32[21,8,8,1]{0,2,3,1:T(8,128)S(1)}, u32[]{:S(2)}, u32[]{:S(2)}) %collective-permute-start.2) | collective-permute-done | bytes 5408 | tf_op jit(solution)/shard_map/ppermute | solution.py:17
  39.1 0.5 %copy.40 = f32[21,8,8,1]{3,0,2,1:T(8,128)S(1)} copy(f32[21,8,8,1]{0,2,3,1:T(8,128)S(1)} %collective-permute-done.2) | data formatting | bytes 10752 | tf_op jit(solution)/shard_map/ppermute | solution.py:17
  39.6 0.0 copy-done.4
  39.6 1.9 %fusion.3 = f32[20,8,8,90]{3,0,2,1:T(8,128)S(1)} fusion(f32[21,8,8,1]{3,0,2,1:T(8,128)S(1)} %copy.42, f32[1,8,8,90]{3,0,2,1:T(1,128)S(1)} %bitcast.82, f32[20,8,8,90]{3,0,2,1:T(8,128)S(1)} %bitcast.71, f32[21,8,8,1]{3,0,2,1:T(8,128)S(1)} %copy.40, f32[8,8,90]{2,1,0:T(8,128)S(1)} %copy.43, f32[8,8,90]{2,1,0:T(8,128)S(1)} %bitcast.87, ...), kind=kOutput, calls=%fused_computation.8 | convolution fusion | flops 30760400 | bytes 1072272 | tf_op jit(solution)/shard_map/bc,clkx->blkx/dot_general | solution.py:111
  41.5 1.0 %copy.44 = f32[20,8,8,90]{3,2,1,0:T(8,128)} copy(f32[20,8,8,90]{3,0,2,1:T(8,128)S(1)} %fusion.3) | data formatting | bytes 921600
  (38 shorter events, 0.8 us)
Async XLA Ops:
  2.4 6.9 %copy-start.1 = (f32[8,2,360]{2,1,0:T(2,128)S(1)}, f32[8,2,360]{2,1,0:T(2,128)}, u32[]{:S(2)}) copy-start(f32[8,2,360]{2,1,0:T(2,128)} %param.12) | copy-start | bytes 69124
  2.5 13.1 %collective-permute-start = (f32[21,1,2,360]{3,1,2,0:T(1,128)S(1)}, f32[21,1,2,360]{3,1,2,0:T(1,128)S(1)}, u32[]{:S(2)}, u32[]{:S(2)}) collective-permute-start(f32[21,1,2,360]{3,1,2,0:T(1,128)S(1)} %get-tuple-element.183), channel_id=1, source_target_pairs={{0,4},{4,8},{8,12},{12,16},{16,20},{20,24},{24,28},{1,5},{5,9},{9,... | collective-permute-start | bytes 181448 | tf_op jit(solution)/shard_map/ppermute | solution.py:17
  5.9 9.7 %collective-permute-start.1 = (f32[21,1,2,360]{3,1,2,0:T(1,128)S(1)}, f32[21,1,2,360]{3,1,2,0:T(1,128)S(1)}, u32[]{:S(2)}, u32[]{:S(2)}) collective-permute-start(f32[21,1,2,360]{3,1,2,0:T(1,128)S(1)} %get-tuple-element.184), channel_id=1, source_target_pairs={{4,0},{8,4},{12,8},{16,12},{20,16},{24,20},{28,24},{5,1},{9,5},{13... | collective-permute-start | bytes 181448 | tf_op jit(solution)/shard_map/ppermute | solution.py:18
  9.3 0.7 %copy-start.2 = (f32[8,2,360]{2,1,0:T(2,128)S(1)}, f32[8,2,360]{2,1,0:T(2,128)}, u32[]{:S(2)}) copy-start(f32[8,2,360]{2,1,0:T(2,128)} %param.13) | copy-start | bytes 69124
  9.4 0.7 %copy-start.5 = (f32[2]{0:T(128)S(1)}, f32[2]{0:T(128)}, u32[]{:S(2)}) copy-start(f32[2]{0:T(128)} %param.14) | copy-start | bytes 28
  17.2 3.6 %copy-start = (f32[8,8,90]{2,1,0:T(8,128)S(1)}, f32[8,8,90]{2,1,0:T(8,128)}, u32[]{:S(2)}) copy-start(f32[8,8,90]{2,1,0:T(8,128)} %param.16) | copy-start | bytes 69124
  17.2 14.5 %all-to-all-start = ((f32[4,22,8,2,90]{4,2,3,1,0:T(8,128)}), f32[4,22,8,2,90]{4,2,3,1,0:T(8,128)S(1)}, u32[]{:S(2)}, u32[]{:S(2)}) async-start(f32[4,22,8,2,90]{4,2,3,1,0:T(8,128)} %pad_maximum_fusion.5), calls=%async_computation | async-start | bytes 1441792 | tf_op jit(solution)/shard_map/all_to_all | solution.py:91
  32.0 0.7 %copy-start.3 = (f32[20]{0:T(128)S(1)}, f32[20]{0:T(128)}, u32[]{:S(2)}) copy-start(f32[20]{0:T(128)} %param.15) | copy-start | bytes 244
  34.5 1.7 %collective-permute-start.3 = (f32[21,8,8,1]{0,2,3,1:T(8,128)S(1)}, f32[21,8,8,1]{0,2,3,1:T(8,128)S(1)}, u32[]{:S(2)}, u32[]{:S(2)}) collective-permute-start(f32[21,8,8,1]{0,2,3,1:T(8,128)S(1)} %copy.41), channel_id=1, source_target_pairs={{1,0},{2,1},{3,2},{0,3},{5,4},{6,5},{7,6},{4,7},{9,8},{10,9},{11,1... | collective-permute-start | bytes 16136 | tf_op jit(solution)/shard_map/ppermute | solution.py:18
  35.7 3.4 %collective-permute-start.2 = (f32[21,8,8,1]{0,2,3,1:T(8,128)S(1)}, f32[21,8,8,1]{0,2,3,1:T(8,128)S(1)}, u32[]{:S(2)}, u32[]{:S(2)}) collective-permute-start(f32[21,8,8,1]{0,2,3,1:T(8,128)S(1)} %copy.39), channel_id=1, source_target_pairs={{0,1},{1,2},{2,3},{3,0},{4,5},{5,6},{6,7},{7,4},{8,9},{9,10},{10,1... | collective-permute-start | bytes 16136 | tf_op jit(solution)/shard_map/ppermute | solution.py:17
  37.0 2.5 %copy-start.4 = (f32[20,20]{1,0:T(8,128)S(1)}, f32[20,20]{1,0:T(8,128)}, u32[]{:S(2)}) copy-start(f32[20,20]{1,0:T(8,128)} %param.17) | copy-start | bytes 4804
